TPU v7x, 32 devices: a whole 2x2x4 slice. The times are simulated.
32 devices in a mesh: dp: 16 (over z, y, x), ctx: 2 (over core).
Axes of the slice: x: 2, y: 2, z: 4, core: 2. Of those that a mesh axis runs over, the one named last changes fastest.
Arguments:
- queries: bfloat16 [4096, 4096], P(('dp', 'ctx')), may hold values from -150 to 150
- keys: bfloat16 [4096, 512], P(('dp', 'ctx')), may hold values from -4 to 4
- values: bfloat16 [4096, 512], P(('dp', 'ctx')), may hold values from -6 to 6
- lengths: int32 [32], replicated, may hold values from 1 to 512, 4096 in all
Outputs:
- attended: bfloat16 [4096, 4096], P(('dp', 'ctx'))
Inputs may be any that keep to these rules, and one draw needn't show every extreme that they name: lengths of the 32 documents sum to 4096; the largest is exactly 512.
All inputs are finite; a program needn't handle non-finite values.
Results may differ from a plain program's by a relative error of at most 0.0045.
Values may be sent and summed in bfloat16 or wider, within the bound.
No kernel may reach another device: no remote copies, remote signals or barrier semaphores. Data moves between devices by JAX's collectives and lax.ppermute only.
A program may use at most 128 MiB of HBM per device.

v0:
```python
import functools
import math

import jax
import jax.numpy as jnp
from jax import lax
from jax.experimental import pallas as pl
from jax.experimental.pallas import tpu as pltpu
from jax.sharding import PartitionSpec as P

HEAD_SIZE = 128
QUERY_HEADS = 32
KEY_VALUE_HEADS = 4
GROUP = QUERY_HEADS // KEY_VALUE_HEADS
HEADS_AT_ONCE = 2
EXCLUDED = -1e30
AXES = ("dp", "ctx")


def plan_kernel(blocks, rows, lengths_ref, places_ref, bias_ref, needed_ref):
    first = places_ref[0]
    query_pos = first + lax.broadcasted_iota(jnp.int32, (rows, rows), 0)

    def later(doc, carried):
        bound, start, first_start = carried
        start = jnp.where(query_pos >= bound, bound, start)
        first_start = jnp.where(first >= bound, bound, first_start)
        return bound + lengths_ref[doc], start, first_start

    zero = jnp.int32(0)
    _, start, first_start = lax.fori_loop(
        0,
        lengths_ref.shape[0],
        later,
        (zero, jnp.zeros((rows, rows), jnp.int32), zero),
        unroll=8,
    )
    needed_ref[0] = 1 + lax.div(first - first_start + (rows - 1), jnp.int32(rows))
    lane = lax.broadcasted_iota(jnp.int32, (rows, rows), 1)
    for b in range(blocks):
        key_pos = first - places_ref[1 + b] * rows + lane
        allowed = key_pos >= start
        if b == 0:
            allowed = allowed & (key_pos <= query_pos)
        bias_ref[:, b * rows : (b + 1) * rows] = jnp.where(
            allowed, jnp.float32(0.0), jnp.float32(EXCLUDED)
        )


def plan(lengths, places, blocks, rows):
    smem = pl.BlockSpec(memory_space=pltpu.SMEM)
    return pl.pallas_call(
        functools.partial(plan_kernel, blocks, rows),
        out_shape=(
            pltpu.VMEM((rows, blocks * rows), jnp.float32),
            jax.ShapeDtypeStruct((1,), jnp.int32),
        ),
        in_specs=[smem, smem],
        out_specs=(pl.BlockSpec(memory_space=pltpu.VMEM), smem),
        cost_estimate=pl.CostEstimate(flops=1000000, bytes_accessed=1000000, transcendentals=0),
    )(lengths, places)


def attention_kernel(blocks, rows, needed_ref, bias_ref, q_ref, key_ref, value_ref, *refs):
    pair_refs = refs[: blocks - 1]
    out_hbm, out_ref, out_sems = refs[blocks - 1 :]
    width = GROUP * HEAD_SIZE
    needed = needed_ref[0]

    def out_copy(g):
        at = pl.ds(pl.multiple_of(g * width, width), width)
        return pltpu.make_async_copy(out_ref.at[:, at], out_hbm.at[:, at], out_sems.at[g])

    factor = jnp.float32(math.log2(math.e) / math.sqrt(HEAD_SIZE))

    def attend(count, g):
        reach = count * rows
        columns = pl.ds(pl.multiple_of(g * HEAD_SIZE, HEAD_SIZE), HEAD_SIZE)
        behind = pair_refs[: count - 1]
        key = jnp.concatenate(
            [key_ref[:, columns]] + [pair[:rows, columns] for pair in behind], axis=0
        )
        value = jnp.concatenate(
            [value_ref[:, columns]] + [pair[rows:, columns] for pair in behind], axis=0
        )
        value = jnp.concatenate([value, jnp.ones((reach, HEAD_SIZE), jnp.bfloat16)], axis=1)
        bias = jnp.concatenate([bias_ref[:, :reach]] * HEADS_AT_ONCE, axis=0)
        for h in range(0, GROUP, HEADS_AT_ONCE):
            heads = [
                pl.ds(pl.multiple_of(g * width + i * HEAD_SIZE, HEAD_SIZE), HEAD_SIZE)
                for i in range(h, h + HEADS_AT_ONCE)
            ]
            q = jnp.concatenate([q_ref[:, at] for at in heads], axis=0)
            scores = lax.dot_general(
                q, key, (((1,), (1,)), ((), ())), preferred_element_type=jnp.float32
            )
            scores = scores + bias
            top = jnp.max(scores, axis=1, keepdims=True)
            weights = jnp.exp2((scores - top) * factor).astype(jnp.bfloat16)
            summed = jnp.dot(weights, value, preferred_element_type=jnp.float32)
            result = (summed[:, :HEAD_SIZE] / summed[:, HEAD_SIZE:]).astype(jnp.bfloat16)
            for n, at in enumerate(heads):
                out_ref[:, at] = result[n * rows : (n + 1) * rows]
        out_copy(g).start()

    for low, count in ((0, 1), (1, 2), (2, blocks)):
        @pl.when((needed > low) & (needed <= count))
        def _():
            def step(g, _):
                attend(count, g)
                return 0

            lax.fori_loop(0, KEY_VALUE_HEADS, step, 0)

    for g in range(KEY_VALUE_HEADS):
        out_copy(g).wait()


def attention(needed, bias, queries, keys, values, pairs):
    rows = queries.shape[0]
    blocks = 1 + len(pairs)
    area = rows * rows * blocks * QUERY_HEADS
    operands = [bias, queries, keys, values, *pairs]
    operands = [pltpu.with_memory_space_constraint(x, pltpu.VMEM) for x in operands]
    return pl.pallas_call(
        functools.partial(attention_kernel, blocks, rows),
        out_shape=jax.ShapeDtypeStruct(queries.shape, queries.dtype),
        in_specs=[pl.BlockSpec(memory_space=pltpu.SMEM)]
        + [pl.BlockSpec(memory_space=pltpu.VMEM)] * len(operands),
        out_specs=pl.BlockSpec(memory_space=pl.ANY),
        scratch_shapes=[
            pltpu.VMEM(queries.shape, queries.dtype),
            pltpu.SemaphoreType.DMA((KEY_VALUE_HEADS,)),
        ],
        compiler_params=pltpu.CompilerParams(vmem_limit_bytes=40 * 1024 * 1024),
        cost_estimate=pl.CostEstimate(
            flops=4 * area * HEAD_SIZE,
            bytes_accessed=4 * (queries.size + blocks * keys.size),
            transcendentals=area,
        ),
    )(needed, *operands)


def per_device(queries, keys, values, lengths):
    rows = queries.shape[0]
    count = lax.axis_size("dp") * lax.axis_size("ctx")
    rounds = lax.axis_size("ctx")
    me = lax.axis_index(AXES)
    is_odd = lax.rem(me, 2) == 1
    own = jnp.concatenate([keys, values], axis=0)

    def back(even, r):
        return 2 * (r + 1) if even else 2 * (rounds - r)

    fetched = []
    for r in range(rounds):
        pairs = [(i - back(i % 2 == 0, r), i) for i in range(count)]
        pairs = [(i, j) for i, j in pairs if i >= 0]
        fetched.append(lax.ppermute(own, AXES, pairs))
    swap = [(i, i ^ 1) for i in range(count)]
    swapped = [lax.ppermute(block, AXES, swap) for block in fetched[:-1]]
    nearest = lax.ppermute(jnp.where(is_odd, fetched[-1], own), AXES, swap)

    behind = [0, 1]
    for r in range(rounds):
        behind.append(jnp.where(is_odd, back(False, r), back(True, r)))
    for r in range(rounds - 1):
        behind.append(jnp.where(is_odd, 1 + back(True, r), back(False, r) - 1))
    places = jnp.stack([me * rows] + [jnp.int32(b) for b in behind]).astype(jnp.int32)
    bias, needed = plan(lengths, places, len(behind), rows)
    return attention(needed, bias, queries, keys, values, [nearest] + fetched + swapped)


def solution(mesh):
    in_specs = (P(AXES, None), P(AXES, None), P(AXES, None), P())
    return jax.shard_map(
        per_device, mesh=mesh, in_specs=in_specs, out_specs=P(AXES, None), check_vma=False
    )
```

profile of v0, /device:TPU:26, one launch (start us, length us, event | category | flops | bytes accessed | tf_op | source)
XLA Modules:
  0.0 27.8 jit_solution(1508691164330100550)
XLA Ops:
  0.0 0.0 copy-start.1
  0.0 0.0 copy-start.2
  0.0 1.0 %constant_dynamic-update-slice_fusion.1 = bf16[256,512]{1,0:T(8,128)(2,1)S(1)} fusion(bf16[128,512]{1,0:T(8,128)(2,1)} %key_ref.1), kind=kLoop, calls=%fused_computation.2 | loop fusion | bytes 262144
  1.0 0.0 copy-done.1
  1.0 3.4 %collective-permute-start.2 = (bf16[256,512]{1,0:T(8,128)(2,1)S(1)}, bf16[256,512]{1,0:T(8,128)(2,1)S(1)}, u32[]{:S(2)}, u32[]{:S(2)}) collective-permute-start(bf16[256,512]{1,0:T(8,128)(2,1)S(1)} %constant_dynamic-update-slice_fusion), channel_id=1, source_target_pairs={{0,2},{2,4},{1,5},{4,6},{3,7},{6,8},{5,9},{8,10},{7,11},{10,12},{9... | collective-permute-start | bytes 786440 | tf_op jit(solution)/shard_map/ppermute | solution.py:159
  4.5 1.9 %collective-permute-start = (bf16[256,512]{1,0:T(8,128)(2,1)S(1)}, bf16[256,512]{1,0:T(8,128)(2,1)S(1)}, u32[]{:S(2)}, u32[]{:S(2)}) collective-permute-start(bf16[256,512]{1,0:T(8,128)(2,1)S(1)} %constant_dynamic-update-slice_fusion), channel_id=1, source_target_pairs={{1,3},{0,4},{3,5},{2,6},{5,7},{4,8},{7,9},{6,10},{9,11},{8,12},{11... | collective-permute-start | bytes 786440 | tf_op jit(solution)/shard_map/ppermute | solution.py:159
  6.4 0.0 copy-start
  6.4 4.0 %collective-permute-done.2.refs_1_ = bf16[256,512]{1,0:T(8,128)(2,1)S(1)} collective-permute-done((bf16[256,512]{1,0:T(8,128)(2,1)S(1)}, bf16[256,512]{1,0:T(8,128)(2,1)S(1)}, u32[]{:S(2)}, u32[]{:S(2)}) %collective-permute-start.2) | collective-permute-done | bytes 262176 | tf_op jit(solution)/shard_map/ppermute | solution.py:159
  10.4 0.2 collective-permute-start.3
  10.6 7.5 %collective-permute-done.refs_2_ = bf16[256,512]{1,0:T(8,128)(2,1)S(1)} collective-permute-done((bf16[256,512]{1,0:T(8,128)(2,1)S(1)}, bf16[256,512]{1,0:T(8,128)(2,1)S(1)}, u32[]{:S(2)}, u32[]{:S(2)}) %collective-permute-start) | collective-permute-done | bytes 262176 | tf_op jit(solution)/shard_map/ppermute | solution.py:159
  18.1 0.1 collective-permute-start.1
  18.2 0.6 %stack.16.places_ref = s32[6]{0:T(128)} concatenate(s32[1]{0:T(128)} %bitcast, s32[1]{0:T(128)} %constant.20.clone.1, s32[1]{0:T(128)} %constant.21.clone.1, s32[1]{0:T(128)} %bitcast.1, s32[1]{0:T(128)} %bitcast.2, s32[1]{0:T(128)} %constant.25.clone.1), dimensions={0} | concatenate | bytes 48 | tf_op jit(solution)/shard_map/stack | solution.py:169
  18.8 1.4 %shard_map.46 = (f32[128,640]{1,0:T(8,128)S(1)}, s32[1]{0:T(128)}) custom-call(s32[32]{0:T(128)} %lengths_ref.1, s32[6]{0:T(128)} %stack.16.places_ref), custom_call_target="tpu_custom_call" | custom-call | flops 1000000 | bytes 1000000 | tf_op jit(solution)/shard_map/pallas_call | solution.py:52
  20.2 0.0 collective-permute-done.3.refs_3_
  20.2 0.0 collective-permute-done.1.refs_0_
  20.2 0.0 copy-done.2
  20.2 0.0 copy-done
  20.2 7.5 %shard_map.47 = bf16[128,4096]{1,0:T(8,128)(2,1)} custom-call(s32[1]{0:T(128)} %get-tuple-element.7.needed_ref, f32[128,640]{1,0:T(8,128)S(1)} %get-tuple-element.8.bias_ref, bf16[128,4096]{1,0:T(8,128)(2,1)S(1)} %copy-done.2, bf16[128,512]{1,0:T(8,128)(2,1)S(1)} %copy-done, bf16[128,512]{1,0:T(8,128)(2,1)S(1)} %copy-done.1, ...), custom_call_target="tpu_custom_call" | custom-call | flops 1342177280 | bytes 3407872 | tf_op jit(solution)/shard_map/pallas_call | solution.py:125
  (2 shorter events, 0.0 us)
Async XLA Ops:
  0.0 1.0 %copy-start.1 = (bf16[128,512]{1,0:T(8,128)(2,1)S(1)}, bf16[128,512]{1,0:T(8,128)(2,1)}, u32[]{:S(2)}) copy-start(bf16[128,512]{1,0:T(8,128)(2,1)} %value_ref.1) | copy-start | bytes 393220
  0.0 20.2 %copy-start.2 = (bf16[128,4096]{1,0:T(8,128)(2,1)S(1)}, bf16[128,4096]{1,0:T(8,128)(2,1)}, u32[]{:S(2)}) copy-start(bf16[128,4096]{1,0:T(8,128)(2,1)} %q_ref.1) | copy-start | bytes 3145732
  1.0 9.3 %collective-permute-start.2 = (bf16[256,512]{1,0:T(8,128)(2,1)S(1)}, bf16[256,512]{1,0:T(8,128)(2,1)S(1)}, u32[]{:S(2)}, u32[]{:S(2)}) collective-permute-start(bf16[256,512]{1,0:T(8,128)(2,1)S(1)} %constant_dynamic-update-slice_fusion), channel_id=1, source_target_pairs={{0,2},{2,4},{1,5},{4,6},{3,7},{6,8},{5,9},{8,10},{7,11},{10,12},{9... | collective-permute-start | bytes 786440 | tf_op jit(solution)/shard_map/ppermute | solution.py:159
  4.5 13.7 %collective-permute-start = (bf16[256,512]{1,0:T(8,128)(2,1)S(1)}, bf16[256,512]{1,0:T(8,128)(2,1)S(1)}, u32[]{:S(2)}, u32[]{:S(2)}) collective-permute-start(bf16[256,512]{1,0:T(8,128)(2,1)S(1)} %constant_dynamic-update-slice_fusion), channel_id=1, source_target_pairs={{1,3},{0,4},{3,5},{2,6},{5,7},{4,8},{7,9},{6,10},{9,11},{8,12},{11... | collective-permute-start | bytes 786440 | tf_op jit(solution)/shard_map/ppermute | solution.py:159
  6.4 13.8 %copy-start = (bf16[128,512]{1,0:T(8,128)(2,1)S(1)}, bf16[128,512]{1,0:T(8,128)(2,1)}, u32[]{:S(2)}) copy-start(bf16[128,512]{1,0:T(8,128)(2,1)} %key_ref.1) | copy-start | bytes 393220
  10.4 9.8 %collective-permute-start.3 = (bf16[256,512]{1,0:T(8,128)(2,1)S(1)}, bf16[256,512]{1,0:T(8,128)(2,1)S(1)}, u32[]{:S(2)}, u32[]{:S(2)}) collective-permute-start(bf16[256,512]{1,0:T(8,128)(2,1)S(1)} %collective-permute-done.2.refs_1_), channel_id=1, source_target_pairs={{0,1},{1,0},{2,3},{3,2},{4,5},{5,4},{6,7},{7,6},{8,9},{9,8},{10,11... | collective-permute-start | bytes 786440 | tf_op jit(solution)/shard_map/ppermute | solution.py:161
  18.1 2.1 %collective-permute-start.1 = (bf16[256,512]{1,0:T(8,128)(2,1)S(1)}, bf16[256,512]{1,0:T(8,128)(2,1)S(1)}, u32[]{:S(2)}, u32[]{:S(2)}) collective-permute-start(bf16[256,512]{1,0:T(8,128)(2,1)S(1)} %broadcast_select_fusion), channel_id=1, source_target_pairs={{0,1},{1,0},{2,3},{3,2},{4,5},{5,4},{6,7},{7,6},{8,9},{9,8},{10,11... | collective-permute-start | bytes 786440 | tf_op jit(solution)/shard_map/ppermute | solution.py:162
where the time goes:
time: 28.3 us; the launch traced here: 27.8 us
  waiting for transfers between devices  11.5 us (41%)
  Pallas kernels  8.9 us (31%)
  starting transfers between devices  5.6 us (20%)
  local copies, waits for them, and re-layouts  1.63 us (6%)
    ppermute x2, waiting for transfers between devices, per_device(): fetched.append(lax.ppermute(own, AXES, pairs))  11.5 us
    pallas_call x1, Pallas kernels, attention(): pl.pallas_call(functools.partial(attention_kernel, blocks, rows), out_sha...  7.54 us
    ppermute x2, starting transfers between devices, per_device(): fetched.append(lax.ppermute(own, AXES, pairs))  5.32 us
    pallas_call x1, Pallas kernels, plan(): pl.pallas_call(functools.partial(plan_kernel, blocks, rows), out_shape=(p...  1.36 us
    unnamed x7, local copies, waits for them, and re-layouts  1.02 us
    another operation x1, local copies, waits for them, and re-layouts, per_device(): jnp.stack([me * rows] + [jnp.int32(b) for b in behind]).astype(jnp.int32)  0.6 us
  transfers between devices with their start and end apart: 4, of which 2 were waited for; matrix products, arithmetic and copies ran while one was open for 2% of the time, Pallas kernels for 5%

commit v1 on v0

v1 whole, which is shorter than its diff:
```python
import functools
import math

import jax
import jax.numpy as jnp
from jax import lax
from jax.experimental import pallas as pl
from jax.experimental.pallas import tpu as pltpu
from jax.sharding import PartitionSpec as P

HEAD_SIZE = 128
QUERY_HEADS = 32
KEY_VALUE_HEADS = 4
GROUP = QUERY_HEADS // KEY_VALUE_HEADS
HEADS_AT_ONCE = 4
EXCLUDED = -1e30
AXES = ("dp", "ctx")


FACTOR = math.log2(math.e) / math.sqrt(HEAD_SIZE)


def head_columns(g, i):
    return pl.ds(pl.multiple_of((g * GROUP + i) * HEAD_SIZE, HEAD_SIZE), HEAD_SIZE)


def stacked(ref, g, heads):
    return jnp.concatenate([ref[:, head_columns(g, i)] for i in heads], axis=0)


def spread(ref, g, heads, rows, value):
    for n, i in enumerate(heads):
        ref[:, head_columns(g, i)] = value[n * rows : (n + 1) * rows].astype(ref.dtype)


def with_ones(value):
    return jnp.concatenate([value, jnp.ones(value.shape, value.dtype)], axis=1)


def scores_of(q, key, bias):
    scores = lax.dot_general(
        q, key, (((1,), (1,)), ((), ())), preferred_element_type=jnp.float32
    )
    return scores + jnp.concatenate([bias] * (q.shape[0] // bias.shape[0]), axis=0)


def weights_of(scores, top):
    return jnp.exp2((scores - top) * jnp.float32(FACTOR)).astype(jnp.bfloat16)


def normalised(summed, total):
    inverse = pl.reciprocal(total, approx=True)
    return summed * (inverse * (2.0 - total * inverse))


def own_kernel(
    rounds, rows, lengths_ref, q_ref, key_ref, value_ref,
    bias_ref, flags_ref, top_ref, total_ref, sum_ref, own_bias_ref,
):
    me = lax.axis_index("dp") * lax.axis_size("ctx") + lax.axis_index("ctx")
    first = me * rows
    query_pos = first + lax.broadcasted_iota(jnp.int32, (rows, rows), 0)

    def later(doc, carried):
        bound, start, first_start = carried
        start = jnp.where(query_pos >= bound, bound, start)
        first_start = jnp.where(first >= bound, bound, first_start)
        return bound + lengths_ref[doc], start, first_start

    zero = jnp.int32(0)
    _, start, first_start = lax.fori_loop(
        0,
        lengths_ref.shape[0],
        later,
        (zero, jnp.zeros((rows, rows), jnp.int32), zero),
        unroll=8,
    )
    odd = lax.rem(me, 2)
    flags_ref[0] = lax.div(first - first_start + (rows - 1), jnp.int32(rows))
    flags_ref[1] = odd
    lane = lax.broadcasted_iota(jnp.int32, (rows, rows), 1)

    def bias_of(allowed):
        return jnp.where(allowed, jnp.float32(0.0), jnp.float32(EXCLUDED))

    for b, behind in enumerate(places_behind(rounds, odd == 1)):
        key_pos = first - behind * rows + lane
        bias_ref[:, b * rows : (b + 1) * rows] = bias_of(key_pos >= start)
    key_pos = first + lane
    own_bias_ref[...] = bias_of((key_pos >= start) & (key_pos <= query_pos))

    def step(g, _):
        key, value = key_ref[:, head_columns(0, g)], value_ref[:, head_columns(0, g)]
        value = with_ones(value)
        for h in range(0, GROUP, HEADS_AT_ONCE):
            heads = range(h, h + HEADS_AT_ONCE)
            scores = scores_of(stacked(q_ref, g, heads), key, own_bias_ref[...])
            top = jnp.max(scores, axis=1, keepdims=True)
            summed = jnp.dot(
                weights_of(scores, top), value, preferred_element_type=jnp.float32
            )
            spread(top_ref, g, heads, rows, jnp.broadcast_to(top, scores.shape))
            spread(sum_ref, g, heads, rows, summed[:, :HEAD_SIZE])
            spread(total_ref, g, heads, rows, summed[:, HEAD_SIZE:])
        return 0

    lax.fori_loop(0, KEY_VALUE_HEADS, step, 0)


def in_vmem(*operands):
    return [pltpu.with_memory_space_constraint(x, pltpu.VMEM) for x in operands]


SMEM = pl.BlockSpec(memory_space=pltpu.SMEM)
VMEM = pl.BlockSpec(memory_space=pltpu.VMEM)


def own_part(lengths, queries, keys, values, rounds):
    rows = queries.shape[0]
    partial = pltpu.VMEM(queries.shape, jnp.float32)
    return pl.pallas_call(
        functools.partial(own_kernel, rounds, rows),
        out_shape=(
            pltpu.VMEM((rows, 2 * rounds * rows), jnp.float32),
            jax.ShapeDtypeStruct((2,), jnp.int32),
            partial,
            partial,
            partial,
        ),
        in_specs=[SMEM, VMEM, VMEM, VMEM],
        out_specs=(VMEM, SMEM, VMEM, VMEM, VMEM),
        scratch_shapes=[pltpu.VMEM((rows, rows), jnp.float32)],
        compiler_params=pltpu.CompilerParams(vmem_limit_bytes=32 * 1024 * 1024),
        cost_estimate=pl.CostEstimate(
            flops=4 * 10**9, bytes_accessed=16 * 10**6, transcendentals=rows * queries.size
        ),
    )(lengths, *in_vmem(queries, keys, values))


def behind_kernel(blocks, rows, flags_ref, bias_ref, q_ref, top_ref, total_ref, sum_ref, *refs):
    pair_refs = refs[:blocks]
    out_hbm, out_ref, out_sems = refs[blocks:]
    width = GROUP * HEAD_SIZE
    needed = flags_ref[0]

    def out_copy(g):
        at = pl.ds(pl.multiple_of(g * width, width), width)
        return pltpu.make_async_copy(out_ref.at[:, at], out_hbm.at[:, at], out_sems.at[g])

    def attend(count, g):
        columns = head_columns(0, g)
        if count:
            key = jnp.concatenate([pair[:rows, columns] for pair in pair_refs[:count]], axis=0)
            value = jnp.concatenate([pair[rows:, columns] for pair in pair_refs[:count]], axis=0)
            value = with_ones(value)
            bias = bias_ref[:, : count * rows]
        for h in range(0, GROUP, HEADS_AT_ONCE):
            heads = range(h, h + HEADS_AT_ONCE)
            summed = stacked(sum_ref, g, heads)
            total = stacked(total_ref, g, heads)
            if count:
                scores = scores_of(stacked(q_ref, g, heads), key, bias)
                own_top = stacked(top_ref, g, heads)
                top = jnp.maximum(own_top, jnp.max(scores, axis=1, keepdims=True))
                fade = jnp.exp2((own_top - top) * jnp.float32(FACTOR))
                more = jnp.dot(
                    weights_of(scores, jnp.concatenate([top] * count, axis=1)),
                    value,
                    preferred_element_type=jnp.float32,
                )
                summed = summed * fade + more[:, :HEAD_SIZE]
                total = total * fade + more[:, HEAD_SIZE:]
            spread(out_ref, g, heads, rows, normalised(summed, total))
        out_copy(g).start()

    for low, count in ((-1, 0), (0, 1), (1, blocks)):
        @pl.when((needed > low) & (needed <= count))
        def _():
            def step(g, _):
                attend(count, g)
                return 0

            lax.fori_loop(0, KEY_VALUE_HEADS, step, 0)

    for g in range(KEY_VALUE_HEADS):
        out_copy(g).wait()


def behind_part(flags, bias, queries, top, total, summed, pairs):
    rows = queries.shape[0]
    area = rows * rows * len(pairs) * QUERY_HEADS
    operands = in_vmem(bias, queries, top, total, summed, *pairs)
    return pl.pallas_call(
        functools.partial(behind_kernel, len(pairs), rows),
        out_shape=jax.ShapeDtypeStruct(queries.shape, queries.dtype),
        in_specs=[SMEM] + [VMEM] * len(operands),
        out_specs=pl.BlockSpec(memory_space=pl.ANY),
        scratch_shapes=[
            pltpu.VMEM(queries.shape, queries.dtype),
            pltpu.SemaphoreType.DMA((KEY_VALUE_HEADS,)),
        ],
        compiler_params=pltpu.CompilerParams(vmem_limit_bytes=32 * 1024 * 1024),
        cost_estimate=pl.CostEstimate(
            flops=4 * area * HEAD_SIZE,
            bytes_accessed=16 * queries.size,
            transcendentals=area,
        ),
    )(flags, *operands)


def fetch_back(rounds, even, r):
    return 2 * (r + 1) if even else 2 * (rounds - r)


def places_behind(rounds, is_odd):
    behind = [1]
    for r in range(rounds):
        behind.append(jnp.where(is_odd, fetch_back(rounds, False, r), fetch_back(rounds, True, r)))
    for r in range(rounds - 1):
        behind.append(
            jnp.where(is_odd, 1 + fetch_back(rounds, True, r), fetch_back(rounds, False, r) - 1)
        )
    return behind


def per_device(queries, keys, values, lengths):
    count = lax.axis_size("dp") * lax.axis_size("ctx")
    rounds = lax.axis_size("ctx")
    own = jnp.concatenate([keys, values], axis=0)

    fetched = []
    for r in range(rounds):
        pairs = [(i - fetch_back(rounds, i % 2 == 0, r), i) for i in range(count)]
        pairs = [(i, j) for i, j in pairs if i >= 0]
        fetched.append(lax.ppermute(own, AXES, pairs))
    bias, flags, top, total, summed = own_part(lengths, queries, keys, values, rounds)
    is_odd = flags[1] == 1
    swap = [(i, i ^ 1) for i in range(count)]
    swapped = [lax.ppermute(block, AXES, swap) for block in fetched[:-1]]
    nearest = lax.ppermute(jnp.where(is_odd, fetched[-1], own), AXES, swap)
    return behind_part(
        flags, bias, queries, top, total, summed, [nearest] + fetched + swapped
    )


def solution(mesh):
    in_specs = (P(AXES, None), P(AXES, None), P(AXES, None), P())
    return jax.shard_map(
        per_device, mesh=mesh, in_specs=in_specs, out_specs=P(AXES, None), check_vma=False
    )
```

time: 28.3 us -> 27.3 us (0.965)
  the two profiles are of different devices: /device:TPU:26 before, /device:TPU:19 now
where the time goes in v1:
time: 27.3 us; the launch traced here: 27.1 us
  Pallas kernels  10.3 us (38%)
  starting transfers between devices  8.74 us (32%)
  local copies, waits for them, and re-layouts  6.1 us (22%)
  waiting for transfers between devices  1.17 us (4%)
  between operations  0.71 us (3%)
    ppermute x2, starting transfers between devices, per_device(): fetched.append(lax.ppermute(own, AXES, pairs))  6.27 us
    pallas_call x1, Pallas kernels, behind_part(): pl.pallas_call(functools.partial(behind_kernel, len(pairs), rows), out_sh...  6.22 us
    unnamed x11, local copies, waits for them, and re-layouts  4.6 us
    pallas_call x1, Pallas kernels, own_part(): pl.pallas_call(functools.partial(own_kernel, rounds, rows), out_shape=(pl...  4.09 us
    ppermute x1, starting transfers between devices, per_device(): swapped = [lax.ppermute(block, AXES, swap) for block in fetched[:-1]]  1.3 us
    ppermute x1, starting transfers between devices, per_device(): nearest = lax.ppermute(jnp.where(is_odd, fetched[-1], own), AXES, swap)  1.18 us
    ppermute x1, waiting for transfers between devices, per_device(): nearest = lax.ppermute(jnp.where(is_odd, fetched[-1], own), AXES, swap)  1.16 us
    concatenate x1, local copies, waits for them, and re-layouts, per_device(): own = jnp.concatenate([keys, values], axis=0)  0.92 us
  transfers between devices with their start and end apart: 4, of which 1 were waited for; matrix products, arithmetic and copies ran while one was open for 2% of the time, Pallas kernels for 15%

profile of v1, /device:TPU:19, one launch (start us, length us, event | category | flops | bytes accessed | tf_op | source)
XLA Modules:
  0.0 27.1 jit_solution(11953635702253175663)
XLA Ops:
  0.0 0.9 %constant_dynamic-update-slice_fusion.1 = bf16[256,512]{1,0:T(8,128)(2,1)S(1)} fusion(bf16[128,512]{1,0:T(8,128)(2,1)} %key_ref.1), kind=kLoop, calls=%fused_computation.2 | loop fusion | bytes 262144
  0.9 0.9 %constant_dynamic-update-slice_fusion = bf16[256,512]{1,0:T(8,128)(2,1)S(1)} fusion(bf16[256,512]{1,0:T(8,128)(2,1)S(1)} %constant_dynamic-update-slice_fusion.1, bf16[128,512]{1,0:T(8,128)(2,1)} %value_ref.1), kind=kLoop, calls=%fused_computation.1 | loop fusion | bytes 262144 | tf_op jit(solution)/shard_map/concatenate | solution.py:229
  1.8 3.1 %collective-permute-start.2 = (bf16[256,512]{1,0:T(8,128)(2,1)S(1)}, bf16[256,512]{1,0:T(8,128)(2,1)S(1)}, u32[]{:S(2)}, u32[]{:S(2)}) collective-permute-start(bf16[256,512]{1,0:T(8,128)(2,1)S(1)} %constant_dynamic-update-slice_fusion), channel_id=1, source_target_pairs={{0,2},{2,4},{1,5},{4,6},{3,7},{6,8},{5,9},{8,10},{7,11},{10,12},{9... | collective-permute-start | bytes 786440 | tf_op jit(solution)/shard_map/ppermute | solution.py:235
  5.0 3.1 %collective-permute-start = (bf16[256,512]{1,0:T(8,128)(2,1)S(1)}, bf16[256,512]{1,0:T(8,128)(2,1)S(1)}, u32[]{:S(2)}, u32[]{:S(2)}) collective-permute-start(bf16[256,512]{1,0:T(8,128)(2,1)S(1)} %constant_dynamic-update-slice_fusion), channel_id=1, source_target_pairs={{1,3},{0,4},{3,5},{2,6},{5,7},{4,8},{7,9},{6,10},{9,11},{8,12},{11... | collective-permute-start | bytes 786440 | tf_op jit(solution)/shard_map/ppermute | solution.py:235
  8.1 0.0 copy-start
  8.1 1.2 %copy-done = bf16[128,4096]{1,0:T(8,128)(2,1)S(1)} copy-done((bf16[128,4096]{1,0:T(8,128)(2,1)S(1)}, bf16[128,4096]{1,0:T(8,128)(2,1)}, u32[]{:S(2)}) %copy-start) | copy-done | bytes 1048600
  9.3 0.0 copy-start.2
  9.3 0.9 %copy-done.2 = bf16[128,512]{1,0:T(8,128)(2,1)S(1)} copy-done((bf16[128,512]{1,0:T(8,128)(2,1)S(1)}, bf16[128,512]{1,0:T(8,128)(2,1)}, u32[]{:S(2)}) %copy-start.2) | copy-done | bytes 131096
  10.3 0.0 copy-start.3
  10.3 0.9 %copy-done.3 = bf16[128,512]{1,0:T(8,128)(2,1)S(1)} copy-done((bf16[128,512]{1,0:T(8,128)(2,1)S(1)}, bf16[128,512]{1,0:T(8,128)(2,1)}, u32[]{:S(2)}) %copy-start.3) | copy-done | bytes 131096
  11.2 0.0 copy-start.4
  11.2 0.7 %copy-done.4 = s32[32]{0:T(128)S(1)} copy-done((s32[32]{0:T(128)S(1)}, s32[32]{0:T(128)}, u32[]{:S(2)}) %copy-start.4) | copy-done | bytes 152
  11.8 0.0 copy-start.1
  11.8 4.1 %shard_map.46 = (f32[128,512]{1,0:T(8,128)S(1)}, s32[2]{0:T(128)S(1)}, f32[128,4096]{1,0:T(8,128)S(1)}, f32[128,4096]{1,0:T(8,128)S(1)}, f32[128,4096]{1,0:T(8,128)S(1)}) custom-call(s32[32]{0:T(128)S(1)} %copy-done.4, bf16[128,4096]{1,0:T(8,128)(2,1)S(1)} %copy-done, bf16[128,512]{1,0:T(8,128)(2,1)S(1)} %copy-done.2, bf16[128,512]{1,0:T(8,128)(2,1)S(1)} %copy-done.3), custom_call_target="tpu_custom_call" | custom-call | flops 4000000000 | bytes 16000000 | tf_op jit(solution)/shard_map/pallas_call | solution.py:121
  15.9 0.6 %slice.3 = s32[1]{0:T(128)} slice(s32[2]{0:T(128)S(1)} %get-tuple-element.10.flags_ref), slice={[1:2]} | slice | bytes 8 | tf_op jit(solution)/shard_map/slice | solution.py:237
  17.1 0.0 collective-permute-done.2.refs_1_
  17.2 1.3 %collective-permute-start.3 = (bf16[256,512]{1,0:T(8,128)(2,1)S(1)}, bf16[256,512]{1,0:T(8,128)(2,1)S(1)}, u32[]{:S(2)}, u32[]{:S(2)}) collective-permute-start(bf16[256,512]{1,0:T(8,128)(2,1)S(1)} %collective-permute-done.2.refs_1_), channel_id=1, source_target_pairs={{0,1},{1,0},{2,3},{3,2},{4,5},{5,4},{6,7},{7,6},{8,9},{9,8},{10,11... | collective-permute-start | bytes 786440 | tf_op jit(solution)/shard_map/ppermute | solution.py:239
  18.5 0.0 collective-permute-done.refs_2_
  18.5 1.2 %collective-permute-start.1 = (bf16[256,512]{1,0:T(8,128)(2,1)S(1)}, bf16[256,512]{1,0:T(8,128)(2,1)S(1)}, u32[]{:S(2)}, u32[]{:S(2)}) collective-permute-start(bf16[256,512]{1,0:T(8,128)(2,1)S(1)} %broadcast_select_fusion), channel_id=1, source_target_pairs={{0,1},{1,0},{2,3},{3,2},{4,5},{5,4},{6,7},{7,6},{8,9},{9,8},{10,11... | collective-permute-start | bytes 786440 | tf_op jit(solution)/shard_map/ppermute | solution.py:240
  19.7 0.0 collective-permute-done.3.refs_3_
  19.7 1.2 %collective-permute-done.1.refs_0_ = bf16[256,512]{1,0:T(8,128)(2,1)S(1)} collective-permute-done((bf16[256,512]{1,0:T(8,128)(2,1)S(1)}, bf16[256,512]{1,0:T(8,128)(2,1)S(1)}, u32[]{:S(2)}, u32[]{:S(2)}) %collective-permute-start.1) | collective-permute-done | bytes 262176 | tf_op jit(solution)/shard_map/ppermute | solution.py:240
  20.8 0.0 copy-done.1
  20.8 6.2 %shard_map.47 = bf16[128,4096]{1,0:T(8,128)(2,1)} custom-call(s32[2]{0:T(128)S(1)} %get-tuple-element.10.flags_ref, f32[128,512]{1,0:T(8,128)S(1)} %get-tuple-element.11.bias_ref, bf16[128,4096]{1,0:T(8,128)(2,1)S(1)} %copy-done.1, f32[128,4096]{1,0:T(8,128)S(1)} %get-tuple-element.12.top_ref, f32[128,4096]{1,0:T(8,128)S(1)} %get-tuple-element.13.total_ref, ...), custom_call_target="tpu_custom_call" | custom-call | flops 1073741824 | bytes 8388608 | tf_op jit(solution)/shard_map/pallas_call | solution.py:193
  (1 shorter events, 0.0 us)
Async XLA Ops:
  1.8 15.3 %collective-permute-start.2 = (bf16[256,512]{1,0:T(8,128)(2,1)S(1)}, bf16[256,512]{1,0:T(8,128)(2,1)S(1)}, u32[]{:S(2)}, u32[]{:S(2)}) collective-permute-start(bf16[256,512]{1,0:T(8,128)(2,1)S(1)} %constant_dynamic-update-slice_fusion), channel_id=1, source_target_pairs={{0,2},{2,4},{1,5},{4,6},{3,7},{6,8},{5,9},{8,10},{7,11},{10,12},{9... | collective-permute-start | bytes 786440 | tf_op jit(solution)/shard_map/ppermute | solution.py:235
  5.0 13.5 %collective-permute-start = (bf16[256,512]{1,0:T(8,128)(2,1)S(1)}, bf16[256,512]{1,0:T(8,128)(2,1)S(1)}, u32[]{:S(2)}, u32[]{:S(2)}) collective-permute-start(bf16[256,512]{1,0:T(8,128)(2,1)S(1)} %constant_dynamic-update-slice_fusion), channel_id=1, source_target_pairs={{1,3},{0,4},{3,5},{2,6},{5,7},{4,8},{7,9},{6,10},{9,11},{8,12},{11... | collective-permute-start | bytes 786440 | tf_op jit(solution)/shard_map/ppermute | solution.py:235
  8.1 1.2 %copy-start = (bf16[128,4096]{1,0:T(8,128)(2,1)S(1)}, bf16[128,4096]{1,0:T(8,128)(2,1)}, u32[]{:S(2)}) copy-start(bf16[128,4096]{1,0:T(8,128)(2,1)} %q_ref.3) | copy-start | bytes 3145732
  9.3 0.9 %copy-start.2 = (bf16[128,512]{1,0:T(8,128)(2,1)S(1)}, bf16[128,512]{1,0:T(8,128)(2,1)}, u32[]{:S(2)}) copy-start(bf16[128,512]{1,0:T(8,128)(2,1)} %key_ref.1) | copy-start | bytes 393220
  10.3 0.9 %copy-start.3 = (bf16[128,512]{1,0:T(8,128)(2,1)S(1)}, bf16[128,512]{1,0:T(8,128)(2,1)}, u32[]{:S(2)}) copy-start(bf16[128,512]{1,0:T(8,128)(2,1)} %value_ref.1) | copy-start | bytes 393220
  11.2 0.7 %copy-start.4 = (s32[32]{0:T(128)S(1)}, s32[32]{0:T(128)}, u32[]{:S(2)}) copy-start(s32[32]{0:T(128)} %lengths_ref.1) | copy-start | bytes 388
  11.8 9.0 %copy-start.1 = (bf16[128,4096]{1,0:T(8,128)(2,1)S(1)}, bf16[128,4096]{1,0:T(8,128)(2,1)}, u32[]{:S(2)}) copy-start(bf16[128,4096]{1,0:T(8,128)(2,1)} %q_ref.3) | copy-start | bytes 3145732
  17.2 2.5 %collective-permute-start.3 = (bf16[256,512]{1,0:T(8,128)(2,1)S(1)}, bf16[256,512]{1,0:T(8,128)(2,1)S(1)}, u32[]{:S(2)}, u32[]{:S(2)}) collective-permute-start(bf16[256,512]{1,0:T(8,128)(2,1)S(1)} %collective-permute-done.2.refs_1_), channel_id=1, source_target_pairs={{0,1},{1,0},{2,3},{3,2},{4,5},{5,4},{6,7},{7,6},{8,9},{9,8},{10,11... | collective-permute-start | bytes 786440 | tf_op jit(solution)/shard_map/ppermute | solution.py:239
  18.5 2.3 %collective-permute-start.1 = (bf16[256,512]{1,0:T(8,128)(2,1)S(1)}, bf16[256,512]{1,0:T(8,128)(2,1)S(1)}, u32[]{:S(2)}, u32[]{:S(2)}) collective-permute-start(bf16[256,512]{1,0:T(8,128)(2,1)S(1)} %broadcast_select_fusion), channel_id=1, source_target_pairs={{0,1},{1,0},{2,3},{3,2},{4,5},{5,4},{6,7},{7,6},{8,9},{9,8},{10,11... | collective-permute-start | bytes 786440 | tf_op jit(solution)/shard_map/ppermute | solution.py:240

commit v2 on v1

v2 whole, which is shorter than its diff:
```python
import functools
import math

import jax
import jax.numpy as jnp
from jax import lax
from jax.experimental import pallas as pl
from jax.experimental.pallas import tpu as pltpu
from jax.sharding import PartitionSpec as P

HEAD_SIZE = 128
QUERY_HEADS = 32
KEY_VALUE_HEADS = 4
GROUP = QUERY_HEADS // KEY_VALUE_HEADS
HEADS_AT_ONCE = 4
EXCLUDED = -1e30
AXES = ("dp", "ctx")


FACTOR = math.log2(math.e) / math.sqrt(HEAD_SIZE)


def head_columns(i):
    return slice(i * HEAD_SIZE, (i + 1) * HEAD_SIZE)


def stacked(ref, heads):
    return jnp.concatenate([ref[:, head_columns(i)] for i in heads], axis=0)


def spread(ref, heads, rows, value):
    for n, i in enumerate(heads):
        ref[:, head_columns(i)] = value[n * rows : (n + 1) * rows].astype(ref.dtype)


def with_ones(value):
    return jnp.concatenate([value, jnp.ones(value.shape, value.dtype)], axis=1)


def scores_of(q, key, bias):
    scores = lax.dot_general(
        q, key, (((1,), (1,)), ((), ())), preferred_element_type=jnp.float32
    )
    return scores + jnp.concatenate([bias] * (q.shape[0] // bias.shape[0]), axis=0)


def weights_of(scores, top):
    return jnp.exp2((scores - top) * jnp.float32(FACTOR)).astype(jnp.bfloat16)


def normalised(summed, total):
    inverse = pl.reciprocal(total, approx=True)
    return summed * (inverse * (2.0 - total * inverse))


def chains():
    return [
        (range(h, h + HEADS_AT_ONCE), h // GROUP) for h in range(0, QUERY_HEADS, HEADS_AT_ONCE)
    ]


def in_turn(*stages):
    runs = chains()
    results = {}
    for turn in range(len(runs) + len(stages) - 1):
        for n, stage in enumerate(stages):
            i = turn - n
            if 0 <= i < len(runs):
                results[i] = stage(*runs[i], *results.pop(i, ()))


def pack_kernel(key_hbm, value_hbm, out_ref, sems):
    rows = key_hbm.shape[0]
    copies = [
        pltpu.make_async_copy(key_hbm, out_ref.at[:rows], sems.at[0]),
        pltpu.make_async_copy(value_hbm, out_ref.at[rows:], sems.at[1]),
    ]
    for copy in copies:
        copy.start()
    for copy in copies:
        copy.wait()


def pack(keys, values):
    rows, width = keys.shape
    return pl.pallas_call(
        pack_kernel,
        out_shape=pltpu.VMEM((2 * rows, width), keys.dtype),
        in_specs=[HBM, HBM],
        out_specs=VMEM,
        scratch_shapes=[pltpu.SemaphoreType.DMA((2,))],
    )(*in_hbm(keys, values))


def own_kernel(
    rounds, rows, own_ref, lengths_hbm, q_hbm,
    bias_ref, flags_ref, odd_ref, q_ref, top_ref, total_ref, sum_ref,
    own_bias_ref, lengths_ref, lengths_sem, q_sems,
):
    lengths_copy = pltpu.make_async_copy(lengths_hbm, lengths_ref, lengths_sem)
    lengths_copy.start()
    width = GROUP * HEAD_SIZE
    q_copies = []
    for g in range(KEY_VALUE_HEADS):
        at = slice(g * width, (g + 1) * width)
        q_copies.append(pltpu.make_async_copy(q_hbm.at[:, at], q_ref.at[:, at], q_sems.at[g]))
        q_copies[g].start()
    me = lax.axis_index("dp") * lax.axis_size("ctx") + lax.axis_index("ctx")
    odd = lax.rem(me, 2)
    odd_ref[...] = jnp.full(odd_ref.shape, odd, jnp.int32)
    first = me * rows
    query_pos = first + lax.broadcasted_iota(jnp.int32, (rows, rows), 0)
    lengths_copy.wait()

    def later(doc, carried):
        bound, start, first_start = carried
        start = jnp.where(query_pos >= bound, bound, start)
        first_start = jnp.where(first >= bound, bound, first_start)
        return bound + lengths_ref[doc], start, first_start

    zero = jnp.int32(0)
    _, start, first_start = lax.fori_loop(
        0,
        lengths_ref.shape[0],
        later,
        (zero, jnp.zeros((rows, rows), jnp.int32), zero),
        unroll=8,
    )
    flags_ref[0] = lax.div(first - first_start + (rows - 1), jnp.int32(rows))
    lane = lax.broadcasted_iota(jnp.int32, (rows, rows), 1)

    def bias_of(allowed):
        return jnp.where(allowed, jnp.float32(0.0), jnp.float32(EXCLUDED))

    key_pos = first + lane
    own_bias_ref[...] = bias_of((key_pos >= start) & (key_pos <= query_pos))
    for b, behind in enumerate(places_behind(rounds, odd == 1)):
        key_pos = first - behind * rows + lane
        bias_ref[:, b * rows : (b + 1) * rows] = bias_of(key_pos >= start)

    def match(heads, g):
        if heads[0] % GROUP == 0:
            q_copies[g].wait()
        return (scores_of(stacked(q_ref, heads), own_ref[:rows, head_columns(g)], own_bias_ref[...]),)

    def weigh(heads, g, scores):
        top = jnp.max(scores, axis=1, keepdims=True)
        spread(top_ref, heads, rows, jnp.broadcast_to(top, scores.shape))
        return (weights_of(scores, top),)

    def gather(heads, g, weights):
        value = with_ones(own_ref[rows:, head_columns(g)])
        summed = jnp.dot(weights, value, preferred_element_type=jnp.float32)
        spread(sum_ref, heads, rows, summed[:, :HEAD_SIZE])
        spread(total_ref, heads, rows, summed[:, HEAD_SIZE:])

    in_turn(match, weigh, gather)


def in_vmem(*operands):
    return [pltpu.with_memory_space_constraint(x, pltpu.VMEM) for x in operands]


def in_hbm(*operands):
    return [pltpu.with_memory_space_constraint(x, pltpu.HBM) for x in operands]


SMEM = pl.BlockSpec(memory_space=pltpu.SMEM)
VMEM = pl.BlockSpec(memory_space=pltpu.VMEM)
HBM = pl.BlockSpec(memory_space=pltpu.HBM)


def own_part(lengths, queries, own, rounds):
    rows = queries.shape[0]
    partial = pltpu.VMEM(queries.shape, jnp.float32)
    return pl.pallas_call(
        functools.partial(own_kernel, rounds, rows),
        out_shape=(
            pltpu.VMEM((rows, 2 * rounds * rows), jnp.float32),
            jax.ShapeDtypeStruct((1,), jnp.int32),
            pltpu.VMEM((1, own.shape[1]), jnp.int32),
            pltpu.VMEM(queries.shape, queries.dtype),
            partial,
            partial,
            partial,
        ),
        in_specs=[VMEM, HBM, HBM],
        out_specs=(VMEM, SMEM, VMEM, VMEM, VMEM, VMEM, VMEM),
        scratch_shapes=[
            pltpu.VMEM((rows, rows), jnp.float32),
            pltpu.SMEM(lengths.shape, jnp.int32),
            pltpu.SemaphoreType.DMA,
            pltpu.SemaphoreType.DMA((KEY_VALUE_HEADS,)),
        ],
        compiler_params=pltpu.CompilerParams(vmem_limit_bytes=32 * 1024 * 1024),
        cost_estimate=pl.CostEstimate(
            flops=4 * 10**9, bytes_accessed=16 * 10**6, transcendentals=rows * queries.size
        ),
    )(*in_vmem(own), *in_hbm(lengths, queries))


def behind_kernel(blocks, rows, flags_ref, bias_ref, q_ref, top_ref, total_ref, sum_ref, *refs):
    pair_refs = refs[:blocks]
    out_hbm, out_ref, out_sems = refs[blocks:]
    width = GROUP * HEAD_SIZE
    needed = flags_ref[0]

    def out_copy(g):
        at = slice(g * width, (g + 1) * width)
        return pltpu.make_async_copy(out_ref.at[:, at], out_hbm.at[:, at], out_sems.at[g])

    def finish(heads, g, summed, total):
        spread(out_ref, heads, rows, normalised(summed, total))
        if heads[-1] % GROUP == GROUP - 1:
            out_copy(g).start()

    def attend(count):
        behind = pair_refs[:count]

        def match(heads, g):
            key = jnp.concatenate([pair[:rows, head_columns(g)] for pair in behind], axis=0)
            return (scores_of(stacked(q_ref, heads), key, bias_ref[:, : count * rows]),)

        def weigh(heads, g, scores):
            own_top = stacked(top_ref, heads)
            top = jnp.maximum(own_top, jnp.max(scores, axis=1, keepdims=True))
            fade = jnp.exp2((own_top - top) * jnp.float32(FACTOR))
            return weights_of(scores, jnp.concatenate([top] * count, axis=1)), fade

        def gather(heads, g, weights, fade):
            value = jnp.concatenate([pair[rows:, head_columns(g)] for pair in behind], axis=0)
            more = jnp.dot(weights, with_ones(value), preferred_element_type=jnp.float32)
            summed = stacked(sum_ref, heads) * fade + more[:, :HEAD_SIZE]
            total = stacked(total_ref, heads) * fade + more[:, HEAD_SIZE:]
            finish(heads, g, summed, total)

        in_turn(match, weigh, gather)

    @pl.when(needed == 0)
    def _():
        in_turn(lambda heads, g: finish(heads, g, stacked(sum_ref, heads), stacked(total_ref, heads)))

    @pl.when(needed == 1)
    def _():
        attend(1)

    @pl.when(needed > 1)
    def _():
        attend(blocks)

    for g in range(KEY_VALUE_HEADS):
        out_copy(g).wait()


def behind_part(flags, bias, queries, top, total, summed, pairs):
    rows = queries.shape[0]
    area = rows * rows * len(pairs) * QUERY_HEADS
    operands = in_vmem(bias, queries, top, total, summed, *pairs)
    return pl.pallas_call(
        functools.partial(behind_kernel, len(pairs), rows),
        out_shape=jax.ShapeDtypeStruct(queries.shape, queries.dtype),
        in_specs=[SMEM] + [VMEM] * len(operands),
        out_specs=HBM,
        scratch_shapes=[
            pltpu.VMEM(queries.shape, queries.dtype),
            pltpu.SemaphoreType.DMA((KEY_VALUE_HEADS,)),
        ],
        compiler_params=pltpu.CompilerParams(vmem_limit_bytes=32 * 1024 * 1024),
        cost_estimate=pl.CostEstimate(
            flops=4 * area * HEAD_SIZE,
            bytes_accessed=16 * queries.size,
            transcendentals=area,
        ),
    )(flags, *operands)


def fetch_back(rounds, even, r):
    return 2 * (r + 1) if even else 2 * (rounds - r)


def places_behind(rounds, is_odd):
    behind = [1]
    for r in range(rounds):
        behind.append(jnp.where(is_odd, fetch_back(rounds, False, r), fetch_back(rounds, True, r)))
    for r in range(rounds - 1):
        behind.append(
            jnp.where(is_odd, 1 + fetch_back(rounds, True, r), fetch_back(rounds, False, r) - 1)
        )
    return behind


def per_device(queries, keys, values, lengths):
    count = lax.axis_size("dp") * lax.axis_size("ctx")
    rounds = lax.axis_size("ctx")
    own = pack(keys, values)

    fetched = []
    for r in range(rounds):
        pairs = [(i - fetch_back(rounds, i % 2 == 0, r), i) for i in range(count)]
        pairs = [(i, j) for i, j in pairs if i >= 0]
        fetched.append(lax.ppermute(own, AXES, pairs))
    bias, flags, odd, queries, top, total, summed = own_part(lengths, queries, own, rounds)
    swap = [(i, i ^ 1) for i in range(count)]
    swapped = [lax.ppermute(block, AXES, swap) for block in fetched[:-1]]
    nearest = lax.ppermute(jnp.where(odd == 1, fetched[-1], own), AXES, swap)
    return behind_part(
        flags, bias, queries, top, total, summed, [nearest] + fetched + swapped
    )


def solution(mesh):
    in_specs = (P(AXES, None), P(AXES, None), P(AXES, None), P())
    return jax.shard_map(
        per_device, mesh=mesh, in_specs=in_specs, out_specs=P(AXES, None), check_vma=False
    )
```

time: 27.3 us -> 25.3 us (0.927)
  local copies, waits for them, and re-layouts: 6.1 us -> 0 us
  starting transfers between devices: 8.74 us -> 13.7 us
  Pallas kernels: 10.3 us -> 8.85 us
  waiting for transfers between devices: 1.17 us -> 2.43 us
  between operations: 0.71 us -> 0.04 us
    ppermute x1, starting transfers between devices: 1.18 us -> 6.74 us  [per_device(): nearest = lax.ppermute(jnp.where(odd == 1, fetched[-1], own), AXES, swap)]
    unnamed x11 -> x0, local copies, waits for them, and re-layouts: 4.6 us -> none
    pallas_call x1, Pallas kernels: 4.09 us -> 2.78 us  [own_part(): pl.pallas_call(functools.partial(own_kernel, rounds, rows), out_shape=(pl...]
    ppermute x2, waiting for transfers between devices: 0.01 us -> 1.27 us  [per_device(): fetched.append(lax.ppermute(own, AXES, pairs))]
    pallas_call x1, Pallas kernels: 6.22 us -> 5.08 us  [behind_part(): pl.pallas_call(functools.partial(behind_kernel, len(pairs), rows), out_sh...]
    pallas_call x0 -> x1, Pallas kernels: none -> 0.98 us  [pack(): pl.pallas_call(pack_kernel, out_shape=pltpu.VMEM((2 * rows, width), keys....]
    concatenate x1 -> x0, local copies, waits for them, and re-layouts: 0.92 us -> none  [per_device(): own = jnp.concatenate([keys, values], axis=0)]
    ppermute x1, starting transfers between devices: 1.3 us -> 0.7 us  [per_device(): swapped = [lax.ppermute(block, AXES, swap) for block in fetched[:-1]]]
  transfers between devices with their start and end apart: 4 -> 4, of which waited for: 1 -> 3; matrix products, arithmetic and copies ran while one was open for 2% -> 0% of each run, Pallas kernels for 15% -> 11%
where the time goes in v2:
time: 25.3 us; the launch traced here: 25.1 us
  starting transfers between devices  13.7 us (54%)
  Pallas kernels  8.85 us (35%)
  waiting for transfers between devices  2.43 us (10%)
    ppermute x1, starting transfers between devices, per_device(): nearest = lax.ppermute(jnp.where(odd == 1, fetched[-1], own), AXES, swap)  6.74 us
    ppermute x2, starting transfers between devices, per_device(): fetched.append(lax.ppermute(own, AXES, pairs))  6.27 us
    pallas_call x1, Pallas kernels, behind_part(): pl.pallas_call(functools.partial(behind_kernel, len(pairs), rows), out_sh...  5.08 us
    pallas_call x1, Pallas kernels, own_part(): pl.pallas_call(functools.partial(own_kernel, rounds, rows), out_shape=(pl...  2.78 us
    ppermute x2, waiting for transfers between devices, per_device(): fetched.append(lax.ppermute(own, AXES, pairs))  1.27 us
    ppermute x1, waiting for transfers between devices, per_device(): nearest = lax.ppermute(jnp.where(odd == 1, fetched[-1], own), AXES, swap)  1.16 us
    pallas_call x1, Pallas kernels, pack(): pl.pallas_call(pack_kernel, out_shape=pltpu.VMEM((2 * rows, width), keys....  0.98 us
    ppermute x1, starting transfers between devices, per_device(): swapped = [lax.ppermute(block, AXES, swap) for block in fetched[:-1]]  0.7 us
  transfers between devices with their start and end apart: 4, of which 3 were waited for; matrix products, arithmetic and copies ran while one was open for 0% of the time, Pallas kernels for 11%

profile of v2, /device:TPU:19, one launch (start us, length us, event | category | flops | bytes accessed | tf_op | source)
XLA Modules:
  0.0 25.1 jit_solution(11674634025423478441)
XLA Ops:
  0.0 1.0 %shard_map.46.own_ref = bf16[256,512]{1,0:T(8,128)(2,1)S(1)} custom-call(bf16[128,512]{1,0:T(8,128)(2,1)} %key_hbm.1, bf16[128,512]{1,0:T(8,128)(2,1)} %value_hbm.1), custom_call_target="tpu_custom_call" | custom-call | tf_op jit(solution)/shard_map/pallas_call | solution.py:86
  1.0 3.1 %collective-permute-start.2 = (bf16[256,512]{1,0:T(8,128)(2,1)S(1)}, bf16[256,512]{1,0:T(8,128)(2,1)S(1)}, u32[]{:S(2)}, u32[]{:S(2)}) collective-permute-start(bf16[256,512]{1,0:T(8,128)(2,1)S(1)} %shard_map.46.own_ref), channel_id=1, source_target_pairs={{0,2},{2,4},{1,5},{4,6},{3,7},{6,8},{5,9},{8,10},{7,11},{10,12},{9... | collective-permute-start | bytes 786440 | tf_op jit(solution)/shard_map/ppermute | solution.py:301
  4.1 3.1 %collective-permute-start = (bf16[256,512]{1,0:T(8,128)(2,1)S(1)}, bf16[256,512]{1,0:T(8,128)(2,1)S(1)}, u32[]{:S(2)}, u32[]{:S(2)}) collective-permute-start(bf16[256,512]{1,0:T(8,128)(2,1)S(1)} %shard_map.46.own_ref), channel_id=1, source_target_pairs={{1,3},{0,4},{3,5},{2,6},{5,7},{4,8},{7,9},{6,10},{9,11},{8,12},{11... | collective-permute-start | bytes 786440 | tf_op jit(solution)/shard_map/ppermute | solution.py:301
  7.3 2.8 %shard_map.47 = (f32[128,512]{1,0:T(8,128)S(1)}, s32[1]{0:T(128)}, s32[1,512]{1,0:T(1,128)S(1)}, bf16[128,4096]{1,0:T(8,128)(2,1)S(1)}, f32[128,4096]{1,0:T(8,12...) custom-call(bf16[256,512]{1,0:T(8,128)(2,1)S(1)} %shard_map.46.own_ref, s32[32]{0:T(128)} %lengths_hbm.1, ...), custom_call_target="tpu_custom_call" | custom-call | flops 4000000000 | bytes 16000000 | tf_op jit(solution)/shard_map/pallas_call | solution.py:176
  10.1 0.6 %collective-permute-done.2.refs_1_ = bf16[256,512]{1,0:T(8,128)(2,1)S(1)} collective-permute-done((bf16[256,512]{1,0:T(8,128)(2,1)S(1)}, bf16[256,512]{1,0:T(8,128)(2,1)S(1)}, u32[]{:S(2)}, u32[]{:S(2)}) %collective-permute-start.2) | collective-permute-done | bytes 262176 | tf_op jit(solution)/shard_map/ppermute | solution.py:301
  10.7 0.7 %collective-permute-start.3 = (bf16[256,512]{1,0:T(8,128)(2,1)S(1)}, bf16[256,512]{1,0:T(8,128)(2,1)S(1)}, u32[]{:S(2)}, u32[]{:S(2)}) collective-permute-start(bf16[256,512]{1,0:T(8,128)(2,1)S(1)} %collective-permute-done.2.refs_1_), channel_id=1, source_target_pairs={{0,1},{1,0},{2,3},{3,2},{4,5},{5,4},{6,7},{7,6},{8,9},{9,8},{10,11... | collective-permute-start | bytes 786440 | tf_op jit(solution)/shard_map/ppermute | solution.py:304
  11.4 0.7 %collective-permute-done.refs_2_ = bf16[256,512]{1,0:T(8,128)(2,1)S(1)} collective-permute-done((bf16[256,512]{1,0:T(8,128)(2,1)S(1)}, bf16[256,512]{1,0:T(8,128)(2,1)S(1)}, u32[]{:S(2)}, u32[]{:S(2)}) %collective-permute-start) | collective-permute-done | bytes 262176 | tf_op jit(solution)/shard_map/ppermute | solution.py:301
  12.1 6.7 %collective-permute-start.1 = (bf16[256,512]{1,0:T(8,128)(2,1)S(1)}, bf16[256,512]{1,0:T(8,128)(2,1)S(1)}, u32[]{:S(2)}, u32[]{:S(2)}) collective-permute-start(bf16[256,512]{1,0:T(8,128)(2,1)S(1)} %broadcast_select_fusion), channel_id=1, source_target_pairs={{0,1},{1,0},{2,3},{3,2},{4,5},{5,4},{6,7},{7,6},{8,9},{9,8},{10,11... | collective-permute-start | bytes 786440 | tf_op jit(solution)/shard_map/ppermute | solution.py:305
  18.8 0.0 collective-permute-done.3.refs_3_
  18.8 1.2 %collective-permute-done.1.refs_0_ = bf16[256,512]{1,0:T(8,128)(2,1)S(1)} collective-permute-done((bf16[256,512]{1,0:T(8,128)(2,1)S(1)}, bf16[256,512]{1,0:T(8,128)(2,1)S(1)}, u32[]{:S(2)}, u32[]{:S(2)}) %collective-permute-start.1) | collective-permute-done | bytes 262176 | tf_op jit(solution)/shard_map/ppermute | solution.py:305
  20.0 5.1 %shard_map.48 = bf16[128,4096]{1,0:T(8,128)(2,1)} custom-call(s32[1]{0:T(128)} %get-tuple-element.12.flags_ref, f32[128,512]{1,0:T(8,128)S(1)} %get-tuple-element.13.bias_ref, bf16[128,4096]{1,0:T(8,128)(2,1)S(1)} %get-tuple-element.14.q_ref, f32[128,4096]{1,0:T(8,128)S(1)} %get-tuple-element.15.top_ref, f32[128,4096]{1,0:T(8,128)S(1)} %get-tuple-element.16.total_ref, ...), custom_call_target="tpu_custom_call" | custom-call | flops 1073741824 | bytes 8388608 | tf_op jit(solution)/shard_map/pallas_call | solution.py:259
  (2 shorter events, 0.1 us)
Async XLA Ops:
  1.0 9.7 %collective-permute-start.2 = (bf16[256,512]{1,0:T(8,128)(2,1)S(1)}, bf16[256,512]{1,0:T(8,128)(2,1)S(1)}, u32[]{:S(2)}, u32[]{:S(2)}) collective-permute-start(bf16[256,512]{1,0:T(8,128)(2,1)S(1)} %shard_map.46.own_ref), channel_id=1, source_target_pairs={{0,2},{2,4},{1,5},{4,6},{3,7},{6,8},{5,9},{8,10},{7,11},{10,12},{9... | collective-permute-start | bytes 786440 | tf_op jit(solution)/shard_map/ppermute | solution.py:301
  4.1 7.9 %collective-permute-start = (bf16[256,512]{1,0:T(8,128)(2,1)S(1)}, bf16[256,512]{1,0:T(8,128)(2,1)S(1)}, u32[]{:S(2)}, u32[]{:S(2)}) collective-permute-start(bf16[256,512]{1,0:T(8,128)(2,1)S(1)} %shard_map.46.own_ref), channel_id=1, source_target_pairs={{1,3},{0,4},{3,5},{2,6},{5,7},{4,8},{7,9},{6,10},{9,11},{8,12},{11... | collective-permute-start | bytes 786440 | tf_op jit(solution)/shard_map/ppermute | solution.py:301
  10.7 8.1 %collective-permute-start.3 = (bf16[256,512]{1,0:T(8,128)(2,1)S(1)}, bf16[256,512]{1,0:T(8,128)(2,1)S(1)}, u32[]{:S(2)}, u32[]{:S(2)}) collective-permute-start(bf16[256,512]{1,0:T(8,128)(2,1)S(1)} %collective-permute-done.2.refs_1_), channel_id=1, source_target_pairs={{0,1},{1,0},{2,3},{3,2},{4,5},{5,4},{6,7},{7,6},{8,9},{9,8},{10,11... | collective-permute-start | bytes 786440 | tf_op jit(solution)/shard_map/ppermute | solution.py:304
  12.1 7.9 %collective-permute-start.1 = (bf16[256,512]{1,0:T(8,128)(2,1)S(1)}, bf16[256,512]{1,0:T(8,128)(2,1)S(1)}, u32[]{:S(2)}, u32[]{:S(2)}) collective-permute-start(bf16[256,512]{1,0:T(8,128)(2,1)S(1)} %broadcast_select_fusion), channel_id=1, source_target_pairs={{0,1},{1,0},{2,3},{3,2},{4,5},{5,4},{6,7},{7,6},{8,9},{9,8},{10,11... | collective-permute-start | bytes 786440 | tf_op jit(solution)/shard_map/ppermute | solution.py:305
